TPU v7x, 32 devices: a whole 2x2x4 slice. The times are simulated.
32 devices in a mesh: fine: 16 (over z, y, x), coarse: 2 (over core).
Axes of the slice: x: 2, y: 2, z: 4, core: 2. Of those that a mesh axis runs over, the one named last changes fastest.
Arguments:
- load_cases: bfloat16 [32, 16, 1024], P(('fine', 'coarse')), may hold values from -6 to 6
- dual_ops: bfloat16 [32, 1024, 1024], P(('fine', 'coarse')), as said below
- coarse_basis: bfloat16 [32, 48, 1024], P(('fine', 'coarse')), may hold values from -0.4375 to 0.4375
- factor_blocks: float32 [32, 4, 48, 48], P(('fine', 'coarse')), may hold values from -0.4375 to 0.4375
- pattern: int32 [32, 4], P(('fine', 'coarse')), may hold values from 0 to 31
- partners: int32 [32, 6], P(('fine', 'coarse')), may hold values from 0 to 15, as said below
- row_counts: int32 [32, 8], P(('fine', 'coarse')), may hold values from 0 to 128, as said below
Outputs:
- multipliers: float32 [32, 16, 1024], P(('fine', 'coarse'))
- residual: float32 [32, 16, 1024], P(('fine', 'coarse'))
Inputs may be any that keep to these rules, and one draw needn't show every extreme that they name: Each layer gives each in-layer block index b its own odd distance d_b, the distances being 1, 3, up to 11 in some order: the subdomain at an even in-layer index i faces (i + d_b) modulo the number of in-layer indices, one at an odd index faces (i - d_b) modulo that number. So the partner of a subdomain's partner is itself, and a subdomain's 6 partners are distinct and differ from itself. `row_counts`: facing blocks have equal counts; blocks 6 of the first layer and 7 of the last layer are 0. `dual_ops`: each subdomain's matrix is symmetric positive definite.
All inputs are finite; a program needn't handle non-finite values.
Results may differ from a plain program's by a relative error of at most 0.0041.
Values may be sent and summed in bfloat16 or wider, within the bound.
No kernel may reach another device: no remote copies, remote signals or barrier semaphores. Data moves between devices by JAX's collectives and lax.ppermute only.
A program may use at most 64 MiB of HBM per device.

v0:
```python
import jax
import jax.numpy as jnp
from jax import lax
from jax.sharding import PartitionSpec as P

PLANES = 6
ITERS = 2


def from_behind(array, axis, by):
    devices = lax.axis_size(axis)
    return lax.ppermute(array, axis, [(i, (i + by) % devices) for i in range(devices)])


def with_halo(array, sides, width):
    for axis, dim in sides:
        devices, length = (lax.axis_size(axis), array.shape[dim])
        up = [(i, (i + 1) % devices) for i in range(devices - 1)]
        down = [(j, i) for i, j in up]
        last = lax.slice_in_dim(array, length - width, length, axis=dim)
        leading = lax.slice_in_dim(array, 0, width, axis=dim)
        before = lax.ppermute(last, axis, up)
        after = lax.ppermute(leading, axis, down)
        array = jnp.concatenate([before, array, after], axis=dim)
    return array


def body(load_cases, dual_ops, coarse_basis, factor_blocks, pattern, partners, row_counts):
    width = load_cases.shape[2]
    block_rows = width // (PLANES + 2)
    fine_count = lax.axis_size("fine")
    fine_index = lax.axis_index("fine")
    partner_row = partners[0]
    count_row = row_counts[0]
    plane_signs = jnp.where(fine_index < partner_row, 1.0, -1.0).astype(jnp.float32)
    block_signs = jnp.concatenate([plane_signs, jnp.array([-1.0, 1.0], jnp.float32)])
    signs = jnp.repeat(block_signs, block_rows)[None, :]
    row_mask = (
        (jnp.arange(block_rows, dtype=jnp.int32)[None, :] < count_row[:, None])
        .astype(jnp.float32)
        .reshape(1, width)
    )
    basis_half = coarse_basis[0]
    basis_full = basis_half.astype(jnp.float32)
    plane_range = jnp.arange(PLANES, dtype=jnp.int32)
    even_side = fine_index % 2 == 0
    distances = 2 * plane_range + 1
    targets = jnp.where(even_side, fine_index + distances, fine_index - distances) % fine_count
    selector = (partner_row[:, None] == targets[None, :]).astype(jnp.bfloat16)

    def assemble(values):
        cases = values.shape[0]
        blocked = values.reshape(cases, PLANES + 2, block_rows)
        in_plane = blocked[:, :PLANES, :]
        outgoing = jnp.einsum(
            "bk,lbr->klr", selector, in_plane, preferred_element_type=jnp.float32
        ).astype(jnp.bfloat16)
        received = []
        for slot in range(PLANES):
            distance = 2 * slot + 1
            arrivals = [
                from_behind(outgoing[slot], "fine", offset) for offset in (-distance, distance)
            ]
            received.append(jnp.where(even_side, arrivals[0], arrivals[1]))
        stacked_in = jnp.stack(received)
        partner_rows = jnp.einsum(
            "bk,klr->blr", selector, stacked_in, preferred_element_type=jnp.float32
        ).astype(jnp.bfloat16)
        stacked = jnp.stack([blocked[:, PLANES, :], blocked[:, PLANES + 1, :]])
        padded = with_halo(stacked, (("coarse", 0),), 1)
        opposite = jnp.concatenate([partner_rows, padded[0:1], padded[3:4]], axis=0)
        opposite = jnp.transpose(opposite, (1, 0, 2)).reshape(cases, width)
        return row_mask * (values.astype(jnp.float32) + opposite.astype(jnp.float32))

    def restrict(values):
        return lax.dot_general(
            signs * values, basis_full, (((1,), (1,)), ((), ())), precision=lax.Precision.HIGHEST
        )

    def gather_coarse(restricted):
        return lax.all_gather(restricted[None], ("fine", "coarse"), axis=0, tiled=True)

    residual = assemble((signs * load_cases[0].astype(jnp.float32)).astype(jnp.bfloat16))
    multipliers = jnp.zeros_like(residual)
    coarse_all = gather_coarse(restrict(residual))
    for iteration in range(ITERS):
        picked = coarse_all[pattern[0]]
        coarse_sol = jnp.einsum(
            "pla,pab->lb", picked, factor_blocks[0], precision=lax.Precision.HIGHEST
        )
        coarse_half = coarse_sol.astype(jnp.bfloat16)
        correction = (
            signs * jnp.dot(coarse_half, basis_half, preferred_element_type=jnp.float32)
        ).astype(jnp.bfloat16)
        direction = residual + assemble(correction)
        scaled = (signs * direction).astype(jnp.bfloat16)
        applied = (signs * jnp.dot(scaled, dual_ops[0], preferred_element_type=jnp.float32)).astype(
            jnp.bfloat16
        )
        image = assemble(applied)
        partials = jnp.stack(
            [jnp.sum(residual * direction, axis=1), jnp.sum(direction * image, axis=1)]
        )
        totals = lax.psum(partials, ("fine", "coarse"))
        step_size = totals[0] / totals[1]
        multipliers = multipliers + step_size[:, None] * direction
        residual = residual - step_size[:, None] * image
        if iteration + 1 < ITERS:
            coarse_all = gather_coarse(restrict(residual))
    return (multipliers[None], residual[None])


def solution(mesh):
    placed = (
        P(("fine", "coarse"), None, None),
        P(("fine", "coarse"), None, None),
        P(("fine", "coarse"), None, None),
        P(("fine", "coarse"), None, None, None),
        P(("fine", "coarse"), None),
        P(("fine", "coarse"), None),
        P(("fine", "coarse"), None),
    )
    return jax.shard_map(
        body,
        mesh=mesh,
        in_specs=placed,
        out_specs=(P(("fine", "coarse"), None, None), P(("fine", "coarse"), None, None)),
        check_vma=False,
    )
```

profile of v0, /device:TPU:1, one launch (start us, length us, event | category | flops | bytes accessed | tf_op | source)
XLA Modules:
  0.0 324.3 jit_solution(4411796309443429698)
XLA Ops:
  0.7 0.8 compare_select_fusion.3
  1.5 0.8 convert_bitcast_fusion
  2.3 0.7 pad_maximum_fusion.2
  3.1 0.9 convolution_convert_fusion.9
  4.1 2.1 collective-permute-start.1
  6.2 4.1 %collective-permute-start = (bf16[16,128]{1,0:T(8,128)(2,1)S(1)}, bf16[16,128]{1,0:T(8,128)(2,1)S(1)}, u32[]{:S(2)}, u32[]{:S(2)}) collective-permute-start(bf16[16,128]{1,0:T(8,128)(2,1)S(1)} %bitcast.414), channel_id=1, source_target_pairs={{0,30},{2,0},{4,2},{6,4},{8,6},{10,8},{12,10},{14,12},{16,14},{18,... | collective-permute-start | bytes 12296 | tf_op jit(solution)/shard_map/ppermute | solution.py:12
  10.2 4.2 %collective-permute-start.2 = (bf16[16,128]{1,0:T(8,128)(2,1)S(1)}, bf16[16,128]{1,0:T(8,128)(2,1)S(1)}, u32[]{:S(2)}, u32[]{:S(2)}) collective-permute-start(bf16[16,128]{1,0:T(8,128)(2,1)S(1)} %bitcast.412), channel_id=1, source_target_pairs={{0,26},{2,28},{4,30},{6,0},{8,2},{10,4},{12,6},{14,8},{16,10},{18,... | collective-permute-start | bytes 12296 | tf_op jit(solution)/shard_map/ppermute | solution.py:12
  14.5 0.7 fusion.97
  15.2 0.7 convert_bitcast_fusion.2
  15.9 4.2 %collective-permute-start.4 = (bf16[16,128]{1,0:T(8,128)(2,1)S(1)}, bf16[16,128]{1,0:T(8,128)(2,1)S(1)}, u32[]{:S(2)}, u32[]{:S(2)}) collective-permute-start(bf16[16,128]{1,0:T(8,128)(2,1)S(1)} %bitcast.408), channel_id=1, source_target_pairs={{0,22},{2,24},{4,26},{6,28},{8,30},{10,0},{12,2},{14,4},{16,6},{18... | collective-permute-start | bytes 12296 | tf_op jit(solution)/shard_map/ppermute | solution.py:12
  20.2 3.3 %collective-permute-start.6 = (bf16[16,128]{1,0:T(8,128)(2,1)S(1)}, bf16[16,128]{1,0:T(8,128)(2,1)S(1)}, u32[]{:S(2)}, u32[]{:S(2)}) collective-permute-start(bf16[16,128]{1,0:T(8,128)(2,1)S(1)} %bitcast.410), channel_id=1, source_target_pairs={{0,18},{2,20},{4,22},{6,24},{8,26},{10,28},{12,30},{14,0},{16,2},{... | collective-permute-start | bytes 12296 | tf_op jit(solution)/shard_map/ppermute | solution.py:12
  23.5 3.2 collective-permute-start.8
  26.9 2.3 collective-permute-start.10
  29.2 1.3 collective-permute-start.12
  30.5 5.7 %collective-permute-start.13 = (bf16[1,16,128]{2,0,1:T(2,128)(2,1)S(1)}, bf16[1,16,128]{2,0,1:T(2,128)(2,1)S(1)}, u32[]{:S(2)}, u32[]{:S(2)}) collective-permute-start(bf16[1,16,128]{2,0,1:T(2,128)(2,1)S(1)} %get-tuple-element.47), channel_id=1, source_target_pairs={{1,0},{3,2},{5,4},{7,6},{9,8},{11,10},{13,12},{15,14},{17,16},{19,... | collective-permute-start | bytes 12296 | tf_op jit(solution)/shard_map/ppermute | solution.py:23
  36.4 0.8 convolution_convert_fusion.8
  37.4 1.1 fusion.26
  38.4 40.2 %all-gather = f32[512,48]{1,0:T(8,128)S(1)} all-gather(f32[16,48]{1,0:T(8,128)S(1)} %fusion.26), channel_id=2, replica_groups=mesh['fine'=16,'coarse'=2] {'fine','coarse'}, dimensions={0}, use_global_device_ids=true | all-gather | bytes 101376 | tf_op jit(solution)/shard_map/all_gather | solution.py:81
  78.6 0.5 gather_fusion
  79.2 1.1 fusion.18
  80.3 1.1 fusion.10
  81.8 5.0 %collective-permute-start.14 = (bf16[16,128]{1,0:T(8,128)(2,1)S(1)}, bf16[16,128]{1,0:T(8,128)(2,1)S(1)}, u32[]{:S(2)}, u32[]{:S(2)}) collective-permute-start(bf16[16,128]{1,0:T(8,128)(2,1)S(1)} %bitcast.432), channel_id=1, source_target_pairs={{0,30},{2,0},{4,2},{6,4},{8,6},{10,8},{12,10},{14,12},{16,14},{18,... | collective-permute-start | bytes 12296 | tf_op jit(solution)/shard_map/ppermute | solution.py:12
  86.9 4.1 %collective-permute-start.16 = (bf16[16,128]{1,0:T(8,128)(2,1)S(1)}, bf16[16,128]{1,0:T(8,128)(2,1)S(1)}, u32[]{:S(2)}, u32[]{:S(2)}) collective-permute-start(bf16[16,128]{1,0:T(8,128)(2,1)S(1)} %bitcast.424), channel_id=1, source_target_pairs={{0,26},{2,28},{4,30},{6,0},{8,2},{10,4},{12,6},{14,8},{16,10},{18,... | collective-permute-start | bytes 12296 | tf_op jit(solution)/shard_map/ppermute | solution.py:12
  91.2 4.1 %collective-permute-start.18 = (bf16[16,128]{1,0:T(8,128)(2,1)S(1)}, bf16[16,128]{1,0:T(8,128)(2,1)S(1)}, u32[]{:S(2)}, u32[]{:S(2)}) collective-permute-start(bf16[16,128]{1,0:T(8,128)(2,1)S(1)} %bitcast.416), channel_id=1, source_target_pairs={{0,22},{2,24},{4,26},{6,28},{8,30},{10,0},{12,2},{14,4},{16,6},{18... | collective-permute-start | bytes 12296 | tf_op jit(solution)/shard_map/ppermute | solution.py:12
  95.4 3.3 %collective-permute-start.20 = (bf16[16,128]{1,0:T(8,128)(2,1)S(1)}, bf16[16,128]{1,0:T(8,128)(2,1)S(1)}, u32[]{:S(2)}, u32[]{:S(2)}) collective-permute-start(bf16[16,128]{1,0:T(8,128)(2,1)S(1)} %bitcast.400), channel_id=1, source_target_pairs={{0,18},{2,20},{4,22},{6,24},{8,26},{10,28},{12,30},{14,0},{16,2},{... | collective-permute-start | bytes 12296 | tf_op jit(solution)/shard_map/ppermute | solution.py:12
  98.7 3.2 collective-permute-start.22
  102.1 2.4 collective-permute-start.24
  104.4 1.3 collective-permute-start.26
  105.7 5.4 %collective-permute-start.27 = (bf16[1,16,128]{2,0,1:T(2,128)(2,1)S(1)}, bf16[1,16,128]{2,0,1:T(2,128)(2,1)S(1)}, u32[]{:S(2)}, u32[]{:S(2)}) collective-permute-start(bf16[1,16,128]{2,0,1:T(2,128)(2,1)S(1)} %get-tuple-element.39), channel_id=1, source_target_pairs={{1,0},{3,2},{5,4},{7,6},{9,8},{11,10},{13,12},{15,14},{17,16},{19,... | collective-permute-start | bytes 12296 | tf_op jit(solution)/shard_map/ppermute | solution.py:23
  111.6 0.4 collective-permute-done.27
  112.1 0.4 fusion.15
  112.9 5.0 %collective-permute-start.28 = (bf16[16,128]{1,0:T(8,128)(2,1)S(1)}, bf16[16,128]{1,0:T(8,128)(2,1)S(1)}, u32[]{:S(2)}, u32[]{:S(2)}) collective-permute-start(bf16[16,128]{1,0:T(8,128)(2,1)S(1)} %bitcast.434), channel_id=1, source_target_pairs={{0,30},{2,0},{4,2},{6,4},{8,6},{10,8},{12,10},{14,12},{16,14},{18,... | collective-permute-start | bytes 12296 | tf_op jit(solution)/shard_map/ppermute | solution.py:12
  118.0 4.1 %collective-permute-start.30 = (bf16[16,128]{1,0:T(8,128)(2,1)S(1)}, bf16[16,128]{1,0:T(8,128)(2,1)S(1)}, u32[]{:S(2)}, u32[]{:S(2)}) collective-permute-start(bf16[16,128]{1,0:T(8,128)(2,1)S(1)} %bitcast.426), channel_id=1, source_target_pairs={{0,26},{2,28},{4,30},{6,0},{8,2},{10,4},{12,6},{14,8},{16,10},{18,... | collective-permute-start | bytes 12296 | tf_op jit(solution)/shard_map/ppermute | solution.py:12
  122.3 4.1 %collective-permute-start.32 = (bf16[16,128]{1,0:T(8,128)(2,1)S(1)}, bf16[16,128]{1,0:T(8,128)(2,1)S(1)}, u32[]{:S(2)}, u32[]{:S(2)}) collective-permute-start(bf16[16,128]{1,0:T(8,128)(2,1)S(1)} %bitcast.418), channel_id=1, source_target_pairs={{0,22},{2,24},{4,26},{6,28},{8,30},{10,0},{12,2},{14,4},{16,6},{18... | collective-permute-start | bytes 12296 | tf_op jit(solution)/shard_map/ppermute | solution.py:12
  126.5 3.3 %collective-permute-start.34 = (bf16[16,128]{1,0:T(8,128)(2,1)S(1)}, bf16[16,128]{1,0:T(8,128)(2,1)S(1)}, u32[]{:S(2)}, u32[]{:S(2)}) collective-permute-start(bf16[16,128]{1,0:T(8,128)(2,1)S(1)} %bitcast.402), channel_id=1, source_target_pairs={{0,18},{2,20},{4,22},{6,24},{8,26},{10,28},{12,30},{14,0},{16,2},{... | collective-permute-start | bytes 12296 | tf_op jit(solution)/shard_map/ppermute | solution.py:12
  129.8 3.2 collective-permute-start.36
  133.2 2.4 collective-permute-start.38
  135.5 1.3 collective-permute-start.40
  136.8 5.6 %collective-permute-start.41 = (bf16[1,16,128]{2,0,1:T(2,128)(2,1)S(1)}, bf16[1,16,128]{2,0,1:T(2,128)(2,1)S(1)}, u32[]{:S(2)}, u32[]{:S(2)}) collective-permute-start(bf16[1,16,128]{2,0,1:T(2,128)(2,1)S(1)} %get-tuple-element.31), channel_id=1, source_target_pairs={{1,0},{3,2},{5,4},{7,6},{9,8},{11,10},{13,12},{15,14},{17,16},{19,... | collective-permute-start | bytes 12296 | tf_op jit(solution)/shard_map/ppermute | solution.py:23
  142.9 0.4 collective-permute-done.41
  143.4 37.6 %psum.14 = f32[2,16]{1,0:T(2,128)S(1)} all-reduce(f32[2,16]{1,0:T(2,128)S(1)} %pad_maximum_fusion), channel_id=1, replica_groups=mesh['fine'=16,'coarse'=2] {'fine','coarse'}, use_global_device_ids=true, to_apply=%region_2.3 | all-reduce | flops 32 | bytes 256 | tf_op jit(solution)/shard_map/psum | solution.py:104
  181.2 41.8 %all-gather.1 = f32[512,48]{1,0:T(8,128)S(1)} all-gather(f32[16,48]{1,0:T(8,128)S(1)} %fusion.23), channel_id=3, replica_groups=mesh['fine'=16,'coarse'=2] {'fine','coarse'}, dimensions={0}, use_global_device_ids=true | all-gather | bytes 101376 | tf_op jit(solution)/shard_map/all_gather | solution.py:81
  223.1 0.5 gather_fusion.1
  224.4 5.0 %collective-permute-start.42 = (bf16[16,128]{1,0:T(8,128)(2,1)S(1)}, bf16[16,128]{1,0:T(8,128)(2,1)S(1)}, u32[]{:S(2)}, u32[]{:S(2)}) collective-permute-start(bf16[16,128]{1,0:T(8,128)(2,1)S(1)} %bitcast.436), channel_id=1, source_target_pairs={{0,30},{2,0},{4,2},{6,4},{8,6},{10,8},{12,10},{14,12},{16,14},{18,... | collective-permute-start | bytes 12296 | tf_op jit(solution)/shard_map/ppermute | solution.py:12
  229.6 4.1 %collective-permute-start.44 = (bf16[16,128]{1,0:T(8,128)(2,1)S(1)}, bf16[16,128]{1,0:T(8,128)(2,1)S(1)}, u32[]{:S(2)}, u32[]{:S(2)}) collective-permute-start(bf16[16,128]{1,0:T(8,128)(2,1)S(1)} %bitcast.428), channel_id=1, source_target_pairs={{0,26},{2,28},{4,30},{6,0},{8,2},{10,4},{12,6},{14,8},{16,10},{18,... | collective-permute-start | bytes 12296 | tf_op jit(solution)/shard_map/ppermute | solution.py:12
  233.8 4.1 %collective-permute-start.46 = (bf16[16,128]{1,0:T(8,128)(2,1)S(1)}, bf16[16,128]{1,0:T(8,128)(2,1)S(1)}, u32[]{:S(2)}, u32[]{:S(2)}) collective-permute-start(bf16[16,128]{1,0:T(8,128)(2,1)S(1)} %bitcast.420), channel_id=1, source_target_pairs={{0,22},{2,24},{4,26},{6,28},{8,30},{10,0},{12,2},{14,4},{16,6},{18... | collective-permute-start | bytes 12296 | tf_op jit(solution)/shard_map/ppermute | solution.py:12
  238.0 3.3 %collective-permute-start.48 = (bf16[16,128]{1,0:T(8,128)(2,1)S(1)}, bf16[16,128]{1,0:T(8,128)(2,1)S(1)}, u32[]{:S(2)}, u32[]{:S(2)}) collective-permute-start(bf16[16,128]{1,0:T(8,128)(2,1)S(1)} %bitcast.404), channel_id=1, source_target_pairs={{0,18},{2,20},{4,22},{6,24},{8,26},{10,28},{12,30},{14,0},{16,2},{... | collective-permute-start | bytes 12296 | tf_op jit(solution)/shard_map/ppermute | solution.py:12
  241.4 3.2 collective-permute-start.50
  244.7 2.4 collective-permute-start.52
  247.1 1.3 collective-permute-start.54
  248.4 5.4 %collective-permute-start.55 = (bf16[1,16,128]{2,0,1:T(2,128)(2,1)S(1)}, bf16[1,16,128]{2,0,1:T(2,128)(2,1)S(1)}, u32[]{:S(2)}, u32[]{:S(2)}) collective-permute-start(bf16[1,16,128]{2,0,1:T(2,128)(2,1)S(1)} %get-tuple-element.23), channel_id=1, source_target_pairs={{1,0},{3,2},{5,4},{7,6},{9,8},{11,10},{13,12},{15,14},{17,16},{19,... | collective-permute-start | bytes 12296 | tf_op jit(solution)/shard_map/ppermute | solution.py:23
  254.2 0.4 collective-permute-done.55
  254.7 0.4 fusion.12
  255.5 5.0 %collective-permute-start.56 = (bf16[16,128]{1,0:T(8,128)(2,1)S(1)}, bf16[16,128]{1,0:T(8,128)(2,1)S(1)}, u32[]{:S(2)}, u32[]{:S(2)}) collective-permute-start(bf16[16,128]{1,0:T(8,128)(2,1)S(1)} %bitcast.438), channel_id=1, source_target_pairs={{0,30},{2,0},{4,2},{6,4},{8,6},{10,8},{12,10},{14,12},{16,14},{18,... | collective-permute-start | bytes 12296 | tf_op jit(solution)/shard_map/ppermute | solution.py:12
  260.6 4.1 %collective-permute-start.58 = (bf16[16,128]{1,0:T(8,128)(2,1)S(1)}, bf16[16,128]{1,0:T(8,128)(2,1)S(1)}, u32[]{:S(2)}, u32[]{:S(2)}) collective-permute-start(bf16[16,128]{1,0:T(8,128)(2,1)S(1)} %bitcast.430), channel_id=1, source_target_pairs={{0,26},{2,28},{4,30},{6,0},{8,2},{10,4},{12,6},{14,8},{16,10},{18,... | collective-permute-start | bytes 12296 | tf_op jit(solution)/shard_map/ppermute | solution.py:12
  264.9 4.1 %collective-permute-start.60 = (bf16[16,128]{1,0:T(8,128)(2,1)S(1)}, bf16[16,128]{1,0:T(8,128)(2,1)S(1)}, u32[]{:S(2)}, u32[]{:S(2)}) collective-permute-start(bf16[16,128]{1,0:T(8,128)(2,1)S(1)} %bitcast.422), channel_id=1, source_target_pairs={{0,22},{2,24},{4,26},{6,28},{8,30},{10,0},{12,2},{14,4},{16,6},{18... | collective-permute-start | bytes 12296 | tf_op jit(solution)/shard_map/ppermute | solution.py:12
  269.0 3.3 %collective-permute-start.62 = (bf16[16,128]{1,0:T(8,128)(2,1)S(1)}, bf16[16,128]{1,0:T(8,128)(2,1)S(1)}, u32[]{:S(2)}, u32[]{:S(2)}) collective-permute-start(bf16[16,128]{1,0:T(8,128)(2,1)S(1)} %bitcast.406), channel_id=1, source_target_pairs={{0,18},{2,20},{4,22},{6,24},{8,26},{10,28},{12,30},{14,0},{16,2},{... | collective-permute-start | bytes 12296 | tf_op jit(solution)/shard_map/ppermute | solution.py:12
  272.4 3.2 collective-permute-start.64
  275.7 2.4 collective-permute-start.66
  278.1 1.3 collective-permute-start.68
  279.4 5.6 %collective-permute-start.69 = (bf16[1,16,128]{2,0,1:T(2,128)(2,1)S(1)}, bf16[1,16,128]{2,0,1:T(2,128)(2,1)S(1)}, u32[]{:S(2)}, u32[]{:S(2)}) collective-permute-start(bf16[1,16,128]{2,0,1:T(2,128)(2,1)S(1)} %get-tuple-element.15), channel_id=1, source_target_pairs={{1,0},{3,2},{5,4},{7,6},{9,8},{11,10},{13,12},{15,14},{17,16},{19,... | collective-permute-start | bytes 12296 | tf_op jit(solution)/shard_map/ppermute | solution.py:23
  285.5 0.4 collective-permute-done.69
  286.0 37.6 %psum.15 = f32[2,16]{1,0:T(2,128)S(1)} all-reduce(f32[2,16]{1,0:T(2,128)S(1)} %pad_maximum_fusion.1), channel_id=1, replica_groups=mesh['fine'=16,'coarse'=2] {'fine','coarse'}, use_global_device_ids=true, to_apply=%region_5.6 | all-reduce | flops 32 | bytes 256 | tf_op jit(solution)/shard_map/psum | solution.py:104
  323.6 0.7 subtract_bitcast_fusion
  (245 shorter events, 6.1 us)
Async XLA Ops:
  4.1 11.8 %collective-permute-start.1 = (bf16[16,128]{1,0:T(8,128)(2,1)S(1)}, bf16[16,128]{1,0:T(8,128)(2,1)S(1)}, u32[]{:S(2)}, u32[]{:S(2)}) collective-permute-start(bf16[16,128]{1,0:T(8,128)(2,1)S(1)} %bitcast.413), channel_id=1, source_target_pairs={{0,2},{2,4},{4,6},{6,8},{8,10},{10,12},{12,14},{14,16},{16,18},{18... | collective-permute-start | bytes 12296 | tf_op jit(solution)/shard_map/ppermute | solution.py:12
  6.2 14.0 %collective-permute-start = (bf16[16,128]{1,0:T(8,128)(2,1)S(1)}, bf16[16,128]{1,0:T(8,128)(2,1)S(1)}, u32[]{:S(2)}, u32[]{:S(2)}) collective-permute-start(bf16[16,128]{1,0:T(8,128)(2,1)S(1)} %bitcast.414), channel_id=1, source_target_pairs={{0,30},{2,0},{4,2},{6,4},{8,6},{10,8},{12,10},{14,12},{16,14},{18,... | collective-permute-start | bytes 12296 | tf_op jit(solution)/shard_map/ppermute | solution.py:12
  10.2 9.9 %collective-permute-start.3 = (bf16[16,128]{1,0:T(8,128)(2,1)S(1)}, bf16[16,128]{1,0:T(8,128)(2,1)S(1)}, u32[]{:S(2)}, u32[]{:S(2)}) collective-permute-start(bf16[16,128]{1,0:T(8,128)(2,1)S(1)} %bitcast.411), channel_id=1, source_target_pairs={{0,6},{2,8},{4,10},{6,12},{8,14},{10,16},{12,18},{14,20},{16,22},{... | collective-permute-start | bytes 12296 | tf_op jit(solution)/shard_map/ppermute | solution.py:12
  10.2 13.2 %collective-permute-start.2 = (bf16[16,128]{1,0:T(8,128)(2,1)S(1)}, bf16[16,128]{1,0:T(8,128)(2,1)S(1)}, u32[]{:S(2)}, u32[]{:S(2)}) collective-permute-start(bf16[16,128]{1,0:T(8,128)(2,1)S(1)} %bitcast.412), channel_id=1, source_target_pairs={{0,26},{2,28},{4,30},{6,0},{8,2},{10,4},{12,6},{14,8},{16,10},{18,... | collective-permute-start | bytes 12296 | tf_op jit(solution)/shard_map/ppermute | solution.py:12
  14.4 9.1 %collective-permute-start.5 = (bf16[16,128]{1,0:T(8,128)(2,1)S(1)}, bf16[16,128]{1,0:T(8,128)(2,1)S(1)}, u32[]{:S(2)}, u32[]{:S(2)}) collective-permute-start(bf16[16,128]{1,0:T(8,128)(2,1)S(1)} %bitcast.407), channel_id=1, source_target_pairs={{0,10},{2,12},{4,14},{6,16},{8,18},{10,20},{12,22},{14,24},{16,26}... | collective-permute-start | bytes 12296 | tf_op jit(solution)/shard_map/ppermute | solution.py:12
  15.9 10.9 %collective-permute-start.4 = (bf16[16,128]{1,0:T(8,128)(2,1)S(1)}, bf16[16,128]{1,0:T(8,128)(2,1)S(1)}, u32[]{:S(2)}, u32[]{:S(2)}) collective-permute-start(bf16[16,128]{1,0:T(8,128)(2,1)S(1)} %bitcast.408), channel_id=1, source_target_pairs={{0,22},{2,24},{4,26},{6,28},{8,30},{10,0},{12,2},{14,4},{16,6},{18... | collective-permute-start | bytes 12296 | tf_op jit(solution)/shard_map/ppermute | solution.py:12
  20.1 6.7 %collective-permute-start.7 = (bf16[16,128]{1,0:T(8,128)(2,1)S(1)}, bf16[16,128]{1,0:T(8,128)(2,1)S(1)}, u32[]{:S(2)}, u32[]{:S(2)}) collective-permute-start(bf16[16,128]{1,0:T(8,128)(2,1)S(1)} %bitcast.409), channel_id=1, source_target_pairs={{0,14},{2,16},{4,18},{6,20},{8,22},{10,24},{12,26},{14,28},{16,30}... | collective-permute-start | bytes 12296 | tf_op jit(solution)/shard_map/ppermute | solution.py:12
  20.2 9.1 %collective-permute-start.6 = (bf16[16,128]{1,0:T(8,128)(2,1)S(1)}, bf16[16,128]{1,0:T(8,128)(2,1)S(1)}, u32[]{:S(2)}, u32[]{:S(2)}) collective-permute-start(bf16[16,128]{1,0:T(8,128)(2,1)S(1)} %bitcast.410), channel_id=1, source_target_pairs={{0,18},{2,20},{4,22},{6,24},{8,26},{10,28},{12,30},{14,0},{16,2},{... | collective-permute-start | bytes 12296 | tf_op jit(solution)/shard_map/ppermute | solution.py:12
  23.5 7.1 %collective-permute-start.9 = (bf16[16,128]{1,0:T(8,128)(2,1)S(1)}, bf16[16,128]{1,0:T(8,128)(2,1)S(1)}, u32[]{:S(2)}, u32[]{:S(2)}) collective-permute-start(bf16[16,128]{1,0:T(8,128)(2,1)S(1)} %bitcast.397), channel_id=1, source_target_pairs={{0,18},{2,20},{4,22},{6,24},{8,26},{10,28},{12,30},{14,0},{16,2},{... | collective-permute-start | bytes 12296 | tf_op jit(solution)/shard_map/ppermute | solution.py:12
  23.5 12.6 %collective-permute-start.8 = (bf16[16,128]{1,0:T(8,128)(2,1)S(1)}, bf16[16,128]{1,0:T(8,128)(2,1)S(1)}, u32[]{:S(2)}, u32[]{:S(2)}) collective-permute-start(bf16[16,128]{1,0:T(8,128)(2,1)S(1)} %bitcast.398), channel_id=1, source_target_pairs={{0,14},{2,16},{4,18},{6,20},{8,22},{10,24},{12,26},{14,28},{16,30}... | collective-permute-start | bytes 12296 | tf_op jit(solution)/shard_map/ppermute | solution.py:12
  26.8 9.5 %collective-permute-start.11 = (bf16[16,128]{1,0:T(8,128)(2,1)S(1)}, bf16[16,128]{1,0:T(8,128)(2,1)S(1)}, u32[]{:S(2)}, u32[]{:S(2)}) collective-permute-start(bf16[16,128]{1,0:T(8,128)(2,1)S(1)} %bitcast.387), channel_id=1, source_target_pairs={{0,22},{2,24},{4,26},{6,28},{8,30},{10,0},{12,2},{14,4},{16,6},{18... | collective-permute-start | bytes 12296 | tf_op jit(solution)/shard_map/ppermute | solution.py:12
  26.9 9.4 %collective-permute-start.10 = (bf16[16,128]{1,0:T(8,128)(2,1)S(1)}, bf16[16,128]{1,0:T(8,128)(2,1)S(1)}, u32[]{:S(2)}, u32[]{:S(2)}) collective-permute-start(bf16[16,128]{1,0:T(8,128)(2,1)S(1)} %bitcast.388), channel_id=1, source_target_pairs={{0,10},{2,12},{4,14},{6,16},{8,18},{10,20},{12,22},{14,24},{16,26}... | collective-permute-start | bytes 12296 | tf_op jit(solution)/shard_map/ppermute | solution.py:12
  29.2 8.1 %collective-permute-start.12 = (bf16[1,16,128]{2,0,1:T(2,128)(2,1)S(1)}, bf16[1,16,128]{2,0,1:T(2,128)(2,1)S(1)}, u32[]{:S(2)}, u32[]{:S(2)}) collective-permute-start(bf16[1,16,128]{2,0,1:T(2,128)(2,1)S(1)} %get-tuple-element.46), channel_id=1, source_target_pairs={{0,1},{2,3},{4,5},{6,7},{8,9},{10,11},{12,13},{14,15},{16,17},{18,... | collective-permute-start | bytes 12296 | tf_op jit(solution)/shard_map/ppermute | solution.py:22
  30.5 6.8 %collective-permute-start.13 = (bf16[1,16,128]{2,0,1:T(2,128)(2,1)S(1)}, bf16[1,16,128]{2,0,1:T(2,128)(2,1)S(1)}, u32[]{:S(2)}, u32[]{:S(2)}) collective-permute-start(bf16[1,16,128]{2,0,1:T(2,128)(2,1)S(1)} %get-tuple-element.47), channel_id=1, source_target_pairs={{1,0},{3,2},{5,4},{7,6},{9,8},{11,10},{13,12},{15,14},{17,16},{19,... | collective-permute-start | bytes 12296 | tf_op jit(solution)/shard_map/ppermute | solution.py:23
  81.7 9.5 %collective-permute-start.15 = (bf16[16,128]{1,0:T(8,128)(2,1)S(1)}, bf16[16,128]{1,0:T(8,128)(2,1)S(1)}, u32[]{:S(2)}, u32[]{:S(2)}) collective-permute-start(bf16[16,128]{1,0:T(8,128)(2,1)S(1)} %bitcast.431), channel_id=1, source_target_pairs={{0,2},{2,4},{4,6},{6,8},{8,10},{10,12},{12,14},{14,16},{16,18},{18... | collective-permute-start | bytes 12296 | tf_op jit(solution)/shard_map/ppermute | solution.py:12
  81.8 13.5 %collective-permute-start.14 = (bf16[16,128]{1,0:T(8,128)(2,1)S(1)}, bf16[16,128]{1,0:T(8,128)(2,1)S(1)}, u32[]{:S(2)}, u32[]{:S(2)}) collective-permute-start(bf16[16,128]{1,0:T(8,128)(2,1)S(1)} %bitcast.432), channel_id=1, source_target_pairs={{0,30},{2,0},{4,2},{6,4},{8,6},{10,8},{12,10},{14,12},{16,14},{18,... | collective-permute-start | bytes 12296 | tf_op jit(solution)/shard_map/ppermute | solution.py:12
  86.9 8.5 %collective-permute-start.17 = (bf16[16,128]{1,0:T(8,128)(2,1)S(1)}, bf16[16,128]{1,0:T(8,128)(2,1)S(1)}, u32[]{:S(2)}, u32[]{:S(2)}) collective-permute-start(bf16[16,128]{1,0:T(8,128)(2,1)S(1)} %bitcast.423), channel_id=1, source_target_pairs={{0,6},{2,8},{4,10},{6,12},{8,14},{10,16},{12,18},{14,20},{16,22},{... | collective-permute-start | bytes 12296 | tf_op jit(solution)/shard_map/ppermute | solution.py:12
  86.9 11.7 %collective-permute-start.16 = (bf16[16,128]{1,0:T(8,128)(2,1)S(1)}, bf16[16,128]{1,0:T(8,128)(2,1)S(1)}, u32[]{:S(2)}, u32[]{:S(2)}) collective-permute-start(bf16[16,128]{1,0:T(8,128)(2,1)S(1)} %bitcast.424), channel_id=1, source_target_pairs={{0,26},{2,28},{4,30},{6,0},{8,2},{10,4},{12,6},{14,8},{16,10},{18,... | collective-permute-start | bytes 12296 | tf_op jit(solution)/shard_map/ppermute | solution.py:12
  91.1 7.6 %collective-permute-start.19 = (bf16[16,128]{1,0:T(8,128)(2,1)S(1)}, bf16[16,128]{1,0:T(8,128)(2,1)S(1)}, u32[]{:S(2)}, u32[]{:S(2)}) collective-permute-start(bf16[16,128]{1,0:T(8,128)(2,1)S(1)} %bitcast.415), channel_id=1, source_target_pairs={{0,10},{2,12},{4,14},{6,16},{8,18},{10,20},{12,22},{14,24},{16,26}... | collective-permute-start | bytes 12296 | tf_op jit(solution)/shard_map/ppermute | solution.py:12
  91.2 10.8 %collective-permute-start.18 = (bf16[16,128]{1,0:T(8,128)(2,1)S(1)}, bf16[16,128]{1,0:T(8,128)(2,1)S(1)}, u32[]{:S(2)}, u32[]{:S(2)}) collective-permute-start(bf16[16,128]{1,0:T(8,128)(2,1)S(1)} %bitcast.416), channel_id=1, source_target_pairs={{0,22},{2,24},{4,26},{6,28},{8,30},{10,0},{12,2},{14,4},{16,6},{18... | collective-permute-start | bytes 12296 | tf_op jit(solution)/shard_map/ppermute | solution.py:12
  95.3 6.7 %collective-permute-start.21 = (bf16[16,128]{1,0:T(8,128)(2,1)S(1)}, bf16[16,128]{1,0:T(8,128)(2,1)S(1)}, u32[]{:S(2)}, u32[]{:S(2)}) collective-permute-start(bf16[16,128]{1,0:T(8,128)(2,1)S(1)} %bitcast.399), channel_id=1, source_target_pairs={{0,14},{2,16},{4,18},{6,20},{8,22},{10,24},{12,26},{14,28},{16,30}... | collective-permute-start | bytes 12296 | tf_op jit(solution)/shard_map/ppermute | solution.py:12
  95.4 9.1 %collective-permute-start.20 = (bf16[16,128]{1,0:T(8,128)(2,1)S(1)}, bf16[16,128]{1,0:T(8,128)(2,1)S(1)}, u32[]{:S(2)}, u32[]{:S(2)}) collective-permute-start(bf16[16,128]{1,0:T(8,128)(2,1)S(1)} %bitcast.400), channel_id=1, source_target_pairs={{0,18},{2,20},{4,22},{6,24},{8,26},{10,28},{12,30},{14,0},{16,2},{... | collective-permute-start | bytes 12296 | tf_op jit(solution)/shard_map/ppermute | solution.py:12
  98.7 7.1 %collective-permute-start.23 = (bf16[16,128]{1,0:T(8,128)(2,1)S(1)}, bf16[16,128]{1,0:T(8,128)(2,1)S(1)}, u32[]{:S(2)}, u32[]{:S(2)}) collective-permute-start(bf16[16,128]{1,0:T(8,128)(2,1)S(1)} %bitcast.389), channel_id=1, source_target_pairs={{0,18},{2,20},{4,22},{6,24},{8,26},{10,28},{12,30},{14,0},{16,2},{... | collective-permute-start | bytes 12296 | tf_op jit(solution)/shard_map/ppermute | solution.py:12
  98.7 12.4 %collective-permute-start.22 = (bf16[16,128]{1,0:T(8,128)(2,1)S(1)}, bf16[16,128]{1,0:T(8,128)(2,1)S(1)}, u32[]{:S(2)}, u32[]{:S(2)}) collective-permute-start(bf16[16,128]{1,0:T(8,128)(2,1)S(1)} %bitcast.390), channel_id=1, source_target_pairs={{0,14},{2,16},{4,18},{6,20},{8,22},{10,24},{12,26},{14,28},{16,30}... | collective-permute-start | bytes 12296 | tf_op jit(solution)/shard_map/ppermute | solution.py:12
  102.0 9.3 %collective-permute-start.25 = (bf16[16,128]{1,0:T(8,128)(2,1)S(1)}, bf16[16,128]{1,0:T(8,128)(2,1)S(1)}, u32[]{:S(2)}, u32[]{:S(2)}) collective-permute-start(bf16[16,128]{1,0:T(8,128)(2,1)S(1)} %bitcast.379), channel_id=1, source_target_pairs={{0,22},{2,24},{4,26},{6,28},{8,30},{10,0},{12,2},{14,4},{16,6},{18... | collective-permute-start | bytes 12296 | tf_op jit(solution)/shard_map/ppermute | solution.py:12
  102.1 9.2 %collective-permute-start.24 = (bf16[16,128]{1,0:T(8,128)(2,1)S(1)}, bf16[16,128]{1,0:T(8,128)(2,1)S(1)}, u32[]{:S(2)}, u32[]{:S(2)}) collective-permute-start(bf16[16,128]{1,0:T(8,128)(2,1)S(1)} %bitcast.380), channel_id=1, source_target_pairs={{0,10},{2,12},{4,14},{6,16},{8,18},{10,20},{12,22},{14,24},{16,26}... | collective-permute-start | bytes 12296 | tf_op jit(solution)/shard_map/ppermute | solution.py:12
  104.4 7.2 %collective-permute-start.26 = (bf16[1,16,128]{2,0,1:T(2,128)(2,1)S(1)}, bf16[1,16,128]{2,0,1:T(2,128)(2,1)S(1)}, u32[]{:S(2)}, u32[]{:S(2)}) collective-permute-start(bf16[1,16,128]{2,0,1:T(2,128)(2,1)S(1)} %get-tuple-element.38), channel_id=1, source_target_pairs={{0,1},{2,3},{4,5},{6,7},{8,9},{10,11},{12,13},{14,15},{16,17},{18,... | collective-permute-start | bytes 12296 | tf_op jit(solution)/shard_map/ppermute | solution.py:22
  112.8 9.5 %collective-permute-start.29 = (bf16[16,128]{1,0:T(8,128)(2,1)S(1)}, bf16[16,128]{1,0:T(8,128)(2,1)S(1)}, u32[]{:S(2)}, u32[]{:S(2)}) collective-permute-start(bf16[16,128]{1,0:T(8,128)(2,1)S(1)} %bitcast.433), channel_id=1, source_target_pairs={{0,2},{2,4},{4,6},{6,8},{8,10},{10,12},{12,14},{14,16},{16,18},{18... | collective-permute-start | bytes 12296 | tf_op jit(solution)/shard_map/ppermute | solution.py:12
  112.9 13.5 %collective-permute-start.28 = (bf16[16,128]{1,0:T(8,128)(2,1)S(1)}, bf16[16,128]{1,0:T(8,128)(2,1)S(1)}, u32[]{:S(2)}, u32[]{:S(2)}) collective-permute-start(bf16[16,128]{1,0:T(8,128)(2,1)S(1)} %bitcast.434), channel_id=1, source_target_pairs={{0,30},{2,0},{4,2},{6,4},{8,6},{10,8},{12,10},{14,12},{16,14},{18,... | collective-permute-start | bytes 12296 | tf_op jit(solution)/shard_map/ppermute | solution.py:12
  118.0 8.5 %collective-permute-start.31 = (bf16[16,128]{1,0:T(8,128)(2,1)S(1)}, bf16[16,128]{1,0:T(8,128)(2,1)S(1)}, u32[]{:S(2)}, u32[]{:S(2)}) collective-permute-start(bf16[16,128]{1,0:T(8,128)(2,1)S(1)} %bitcast.425), channel_id=1, source_target_pairs={{0,6},{2,8},{4,10},{6,12},{8,14},{10,16},{12,18},{14,20},{16,22},{... | collective-permute-start | bytes 12296 | tf_op jit(solution)/shard_map/ppermute | solution.py:12
  118.0 11.7 %collective-permute-start.30 = (bf16[16,128]{1,0:T(8,128)(2,1)S(1)}, bf16[16,128]{1,0:T(8,128)(2,1)S(1)}, u32[]{:S(2)}, u32[]{:S(2)}) collective-permute-start(bf16[16,128]{1,0:T(8,128)(2,1)S(1)} %bitcast.426), channel_id=1, source_target_pairs={{0,26},{2,28},{4,30},{6,0},{8,2},{10,4},{12,6},{14,8},{16,10},{18,... | collective-permute-start | bytes 12296 | tf_op jit(solution)/shard_map/ppermute | solution.py:12
  122.2 7.6 %collective-permute-start.33 = (bf16[16,128]{1,0:T(8,128)(2,1)S(1)}, bf16[16,128]{1,0:T(8,128)(2,1)S(1)}, u32[]{:S(2)}, u32[]{:S(2)}) collective-permute-start(bf16[16,128]{1,0:T(8,128)(2,1)S(1)} %bitcast.417), channel_id=1, source_target_pairs={{0,10},{2,12},{4,14},{6,16},{8,18},{10,20},{12,22},{14,24},{16,26}... | collective-permute-start | bytes 12296 | tf_op jit(solution)/shard_map/ppermute | solution.py:12
  122.3 10.8 %collective-permute-start.32 = (bf16[16,128]{1,0:T(8,128)(2,1)S(1)}, bf16[16,128]{1,0:T(8,128)(2,1)S(1)}, u32[]{:S(2)}, u32[]{:S(2)}) collective-permute-start(bf16[16,128]{1,0:T(8,128)(2,1)S(1)} %bitcast.418), channel_id=1, source_target_pairs={{0,22},{2,24},{4,26},{6,28},{8,30},{10,0},{12,2},{14,4},{16,6},{18... | collective-permute-start | bytes 12296 | tf_op jit(solution)/shard_map/ppermute | solution.py:12
  126.4 6.7 %collective-permute-start.35 = (bf16[16,128]{1,0:T(8,128)(2,1)S(1)}, bf16[16,128]{1,0:T(8,128)(2,1)S(1)}, u32[]{:S(2)}, u32[]{:S(2)}) collective-permute-start(bf16[16,128]{1,0:T(8,128)(2,1)S(1)} %bitcast.401), channel_id=1, source_target_pairs={{0,14},{2,16},{4,18},{6,20},{8,22},{10,24},{12,26},{14,28},{16,30}... | collective-permute-start | bytes 12296 | tf_op jit(solution)/shard_map/ppermute | solution.py:12
  126.5 9.1 %collective-permute-start.34 = (bf16[16,128]{1,0:T(8,128)(2,1)S(1)}, bf16[16,128]{1,0:T(8,128)(2,1)S(1)}, u32[]{:S(2)}, u32[]{:S(2)}) collective-permute-start(bf16[16,128]{1,0:T(8,128)(2,1)S(1)} %bitcast.402), channel_id=1, source_target_pairs={{0,18},{2,20},{4,22},{6,24},{8,26},{10,28},{12,30},{14,0},{16,2},{... | collective-permute-start | bytes 12296 | tf_op jit(solution)/shard_map/ppermute | solution.py:12
  129.8 7.1 %collective-permute-start.37 = (bf16[16,128]{1,0:T(8,128)(2,1)S(1)}, bf16[16,128]{1,0:T(8,128)(2,1)S(1)}, u32[]{:S(2)}, u32[]{:S(2)}) collective-permute-start(bf16[16,128]{1,0:T(8,128)(2,1)S(1)} %bitcast.391), channel_id=1, source_target_pairs={{0,18},{2,20},{4,22},{6,24},{8,26},{10,28},{12,30},{14,0},{16,2},{... | collective-permute-start | bytes 12296 | tf_op jit(solution)/shard_map/ppermute | solution.py:12
  129.8 12.6 %collective-permute-start.36 = (bf16[16,128]{1,0:T(8,128)(2,1)S(1)}, bf16[16,128]{1,0:T(8,128)(2,1)S(1)}, u32[]{:S(2)}, u32[]{:S(2)}) collective-permute-start(bf16[16,128]{1,0:T(8,128)(2,1)S(1)} %bitcast.392), channel_id=1, source_target_pairs={{0,14},{2,16},{4,18},{6,20},{8,22},{10,24},{12,26},{14,28},{16,30}... | collective-permute-start | bytes 12296 | tf_op jit(solution)/shard_map/ppermute | solution.py:12
  133.1 9.5 %collective-permute-start.39 = (bf16[16,128]{1,0:T(8,128)(2,1)S(1)}, bf16[16,128]{1,0:T(8,128)(2,1)S(1)}, u32[]{:S(2)}, u32[]{:S(2)}) collective-permute-start(bf16[16,128]{1,0:T(8,128)(2,1)S(1)} %bitcast.381), channel_id=1, source_target_pairs={{0,22},{2,24},{4,26},{6,28},{8,30},{10,0},{12,2},{14,4},{16,6},{18... | collective-permute-start | bytes 12296 | tf_op jit(solution)/shard_map/ppermute | solution.py:12
  133.2 9.4 %collective-permute-start.38 = (bf16[16,128]{1,0:T(8,128)(2,1)S(1)}, bf16[16,128]{1,0:T(8,128)(2,1)S(1)}, u32[]{:S(2)}, u32[]{:S(2)}) collective-permute-start(bf16[16,128]{1,0:T(8,128)(2,1)S(1)} %bitcast.382), channel_id=1, source_target_pairs={{0,10},{2,12},{4,14},{6,16},{8,18},{10,20},{12,22},{14,24},{16,26}... | collective-permute-start | bytes 12296 | tf_op jit(solution)/shard_map/ppermute | solution.py:12
  135.5 7.4 %collective-permute-start.40 = (bf16[1,16,128]{2,0,1:T(2,128)(2,1)S(1)}, bf16[1,16,128]{2,0,1:T(2,128)(2,1)S(1)}, u32[]{:S(2)}, u32[]{:S(2)}) collective-permute-start(bf16[1,16,128]{2,0,1:T(2,128)(2,1)S(1)} %get-tuple-element.30), channel_id=1, source_target_pairs={{0,1},{2,3},{4,5},{6,7},{8,9},{10,11},{12,13},{14,15},{16,17},{18,... | collective-permute-start | bytes 12296 | tf_op jit(solution)/shard_map/ppermute | solution.py:22
  224.4 9.5 %collective-permute-start.43 = (bf16[16,128]{1,0:T(8,128)(2,1)S(1)}, bf16[16,128]{1,0:T(8,128)(2,1)S(1)}, u32[]{:S(2)}, u32[]{:S(2)}) collective-permute-start(bf16[16,128]{1,0:T(8,128)(2,1)S(1)} %bitcast.435), channel_id=1, source_target_pairs={{0,2},{2,4},{4,6},{6,8},{8,10},{10,12},{12,14},{14,16},{16,18},{18... | collective-permute-start | bytes 12296 | tf_op jit(solution)/shard_map/ppermute | solution.py:12
  224.4 13.5 %collective-permute-start.42 = (bf16[16,128]{1,0:T(8,128)(2,1)S(1)}, bf16[16,128]{1,0:T(8,128)(2,1)S(1)}, u32[]{:S(2)}, u32[]{:S(2)}) collective-permute-start(bf16[16,128]{1,0:T(8,128)(2,1)S(1)} %bitcast.436), channel_id=1, source_target_pairs={{0,30},{2,0},{4,2},{6,4},{8,6},{10,8},{12,10},{14,12},{16,14},{18,... | collective-permute-start | bytes 12296 | tf_op jit(solution)/shard_map/ppermute | solution.py:12
  229.5 8.5 %collective-permute-start.45 = (bf16[16,128]{1,0:T(8,128)(2,1)S(1)}, bf16[16,128]{1,0:T(8,128)(2,1)S(1)}, u32[]{:S(2)}, u32[]{:S(2)}) collective-permute-start(bf16[16,128]{1,0:T(8,128)(2,1)S(1)} %bitcast.427), channel_id=1, source_target_pairs={{0,6},{2,8},{4,10},{6,12},{8,14},{10,16},{12,18},{14,20},{16,22},{... | collective-permute-start | bytes 12296 | tf_op jit(solution)/shard_map/ppermute | solution.py:12
  229.6 11.7 %collective-permute-start.44 = (bf16[16,128]{1,0:T(8,128)(2,1)S(1)}, bf16[16,128]{1,0:T(8,128)(2,1)S(1)}, u32[]{:S(2)}, u32[]{:S(2)}) collective-permute-start(bf16[16,128]{1,0:T(8,128)(2,1)S(1)} %bitcast.428), channel_id=1, source_target_pairs={{0,26},{2,28},{4,30},{6,0},{8,2},{10,4},{12,6},{14,8},{16,10},{18,... | collective-permute-start | bytes 12296 | tf_op jit(solution)/shard_map/ppermute | solution.py:12
  233.8 7.6 %collective-permute-start.47 = (bf16[16,128]{1,0:T(8,128)(2,1)S(1)}, bf16[16,128]{1,0:T(8,128)(2,1)S(1)}, u32[]{:S(2)}, u32[]{:S(2)}) collective-permute-start(bf16[16,128]{1,0:T(8,128)(2,1)S(1)} %bitcast.419), channel_id=1, source_target_pairs={{0,10},{2,12},{4,14},{6,16},{8,18},{10,20},{12,22},{14,24},{16,26}... | collective-permute-start | bytes 12296 | tf_op jit(solution)/shard_map/ppermute | solution.py:12
  233.8 10.8 %collective-permute-start.46 = (bf16[16,128]{1,0:T(8,128)(2,1)S(1)}, bf16[16,128]{1,0:T(8,128)(2,1)S(1)}, u32[]{:S(2)}, u32[]{:S(2)}) collective-permute-start(bf16[16,128]{1,0:T(8,128)(2,1)S(1)} %bitcast.420), channel_id=1, source_target_pairs={{0,22},{2,24},{4,26},{6,28},{8,30},{10,0},{12,2},{14,4},{16,6},{18... | collective-permute-start | bytes 12296 | tf_op jit(solution)/shard_map/ppermute | solution.py:12
  238.0 9.1 %collective-permute-start.48 = (bf16[16,128]{1,0:T(8,128)(2,1)S(1)}, bf16[16,128]{1,0:T(8,128)(2,1)S(1)}, u32[]{:S(2)}, u32[]{:S(2)}) collective-permute-start(bf16[16,128]{1,0:T(8,128)(2,1)S(1)} %bitcast.404), channel_id=1, source_target_pairs={{0,18},{2,20},{4,22},{6,24},{8,26},{10,28},{12,30},{14,0},{16,2},{... | collective-permute-start | bytes 12296 | tf_op jit(solution)/shard_map/ppermute | solution.py:12
  241.3 7.1 %collective-permute-start.51 = (bf16[16,128]{1,0:T(8,128)(2,1)S(1)}, bf16[16,128]{1,0:T(8,128)(2,1)S(1)}, u32[]{:S(2)}, u32[]{:S(2)}) collective-permute-start(bf16[16,128]{1,0:T(8,128)(2,1)S(1)} %bitcast.393), channel_id=1, source_target_pairs={{0,18},{2,20},{4,22},{6,24},{8,26},{10,28},{12,30},{14,0},{16,2},{... | collective-permute-start | bytes 12296 | tf_op jit(solution)/shard_map/ppermute | solution.py:12
  241.4 12.4 %collective-permute-start.50 = (bf16[16,128]{1,0:T(8,128)(2,1)S(1)}, bf16[16,128]{1,0:T(8,128)(2,1)S(1)}, u32[]{:S(2)}, u32[]{:S(2)}) collective-permute-start(bf16[16,128]{1,0:T(8,128)(2,1)S(1)} %bitcast.394), channel_id=1, source_target_pairs={{0,14},{2,16},{4,18},{6,20},{8,22},{10,24},{12,26},{14,28},{16,30}... | collective-permute-start | bytes 12296 | tf_op jit(solution)/shard_map/ppermute | solution.py:12
  244.6 9.3 %collective-permute-start.53 = (bf16[16,128]{1,0:T(8,128)(2,1)S(1)}, bf16[16,128]{1,0:T(8,128)(2,1)S(1)}, u32[]{:S(2)}, u32[]{:S(2)}) collective-permute-start(bf16[16,128]{1,0:T(8,128)(2,1)S(1)} %bitcast.383), channel_id=1, source_target_pairs={{0,22},{2,24},{4,26},{6,28},{8,30},{10,0},{12,2},{14,4},{16,6},{18... | collective-permute-start | bytes 12296 | tf_op jit(solution)/shard_map/ppermute | solution.py:12
  244.7 9.2 %collective-permute-start.52 = (bf16[16,128]{1,0:T(8,128)(2,1)S(1)}, bf16[16,128]{1,0:T(8,128)(2,1)S(1)}, u32[]{:S(2)}, u32[]{:S(2)}) collective-permute-start(bf16[16,128]{1,0:T(8,128)(2,1)S(1)} %bitcast.384), channel_id=1, source_target_pairs={{0,10},{2,12},{4,14},{6,16},{8,18},{10,20},{12,22},{14,24},{16,26}... | collective-permute-start | bytes 12296 | tf_op jit(solution)/shard_map/ppermute | solution.py:12
  247.1 7.2 %collective-permute-start.54 = (bf16[1,16,128]{2,0,1:T(2,128)(2,1)S(1)}, bf16[1,16,128]{2,0,1:T(2,128)(2,1)S(1)}, u32[]{:S(2)}, u32[]{:S(2)}) collective-permute-start(bf16[1,16,128]{2,0,1:T(2,128)(2,1)S(1)} %get-tuple-element.22), channel_id=1, source_target_pairs={{0,1},{2,3},{4,5},{6,7},{8,9},{10,11},{12,13},{14,15},{16,17},{18,... | collective-permute-start | bytes 12296 | tf_op jit(solution)/shard_map/ppermute | solution.py:22
  255.4 9.5 %collective-permute-start.57 = (bf16[16,128]{1,0:T(8,128)(2,1)S(1)}, bf16[16,128]{1,0:T(8,128)(2,1)S(1)}, u32[]{:S(2)}, u32[]{:S(2)}) collective-permute-start(bf16[16,128]{1,0:T(8,128)(2,1)S(1)} %bitcast.437), channel_id=1, source_target_pairs={{0,2},{2,4},{4,6},{6,8},{8,10},{10,12},{12,14},{14,16},{16,18},{18... | collective-permute-start | bytes 12296 | tf_op jit(solution)/shard_map/ppermute | solution.py:12
  255.5 13.5 %collective-permute-start.56 = (bf16[16,128]{1,0:T(8,128)(2,1)S(1)}, bf16[16,128]{1,0:T(8,128)(2,1)S(1)}, u32[]{:S(2)}, u32[]{:S(2)}) collective-permute-start(bf16[16,128]{1,0:T(8,128)(2,1)S(1)} %bitcast.438), channel_id=1, source_target_pairs={{0,30},{2,0},{4,2},{6,4},{8,6},{10,8},{12,10},{14,12},{16,14},{18,... | collective-permute-start | bytes 12296 | tf_op jit(solution)/shard_map/ppermute | solution.py:12
  260.6 8.5 %collective-permute-start.59 = (bf16[16,128]{1,0:T(8,128)(2,1)S(1)}, bf16[16,128]{1,0:T(8,128)(2,1)S(1)}, u32[]{:S(2)}, u32[]{:S(2)}) collective-permute-start(bf16[16,128]{1,0:T(8,128)(2,1)S(1)} %bitcast.429), channel_id=1, source_target_pairs={{0,6},{2,8},{4,10},{6,12},{8,14},{10,16},{12,18},{14,20},{16,22},{... | collective-permute-start | bytes 12296 | tf_op jit(solution)/shard_map/ppermute | solution.py:12
  260.6 11.7 %collective-permute-start.58 = (bf16[16,128]{1,0:T(8,128)(2,1)S(1)}, bf16[16,128]{1,0:T(8,128)(2,1)S(1)}, u32[]{:S(2)}, u32[]{:S(2)}) collective-permute-start(bf16[16,128]{1,0:T(8,128)(2,1)S(1)} %bitcast.430), channel_id=1, source_target_pairs={{0,26},{2,28},{4,30},{6,0},{8,2},{10,4},{12,6},{14,8},{16,10},{18,... | collective-permute-start | bytes 12296 | tf_op jit(solution)/shard_map/ppermute | solution.py:12
  264.8 7.6 %collective-permute-start.61 = (bf16[16,128]{1,0:T(8,128)(2,1)S(1)}, bf16[16,128]{1,0:T(8,128)(2,1)S(1)}, u32[]{:S(2)}, u32[]{:S(2)}) collective-permute-start(bf16[16,128]{1,0:T(8,128)(2,1)S(1)} %bitcast.421), channel_id=1, source_target_pairs={{0,10},{2,12},{4,14},{6,16},{8,18},{10,20},{12,22},{14,24},{16,26}... | collective-permute-start | bytes 12296 | tf_op jit(solution)/shard_map/ppermute | solution.py:12
  264.9 10.8 %collective-permute-start.60 = (bf16[16,128]{1,0:T(8,128)(2,1)S(1)}, bf16[16,128]{1,0:T(8,128)(2,1)S(1)}, u32[]{:S(2)}, u32[]{:S(2)}) collective-permute-start(bf16[16,128]{1,0:T(8,128)(2,1)S(1)} %bitcast.422), channel_id=1, source_target_pairs={{0,22},{2,24},{4,26},{6,28},{8,30},{10,0},{12,2},{14,4},{16,6},{18... | collective-permute-start | bytes 12296 | tf_op jit(solution)/shard_map/ppermute | solution.py:12
  269.0 9.1 %collective-permute-start.62 = (bf16[16,128]{1,0:T(8,128)(2,1)S(1)}, bf16[16,128]{1,0:T(8,128)(2,1)S(1)}, u32[]{:S(2)}, u32[]{:S(2)}) collective-permute-start(bf16[16,128]{1,0:T(8,128)(2,1)S(1)} %bitcast.406), channel_id=1, source_target_pairs={{0,18},{2,20},{4,22},{6,24},{8,26},{10,28},{12,30},{14,0},{16,2},{... | collective-permute-start | bytes 12296 | tf_op jit(solution)/shard_map/ppermute | solution.py:12
  272.3 7.1 %collective-permute-start.65 = (bf16[16,128]{1,0:T(8,128)(2,1)S(1)}, bf16[16,128]{1,0:T(8,128)(2,1)S(1)}, u32[]{:S(2)}, u32[]{:S(2)}) collective-permute-start(bf16[16,128]{1,0:T(8,128)(2,1)S(1)} %bitcast.395), channel_id=1, source_target_pairs={{0,18},{2,20},{4,22},{6,24},{8,26},{10,28},{12,30},{14,0},{16,2},{... | collective-permute-start | bytes 12296 | tf_op jit(solution)/shard_map/ppermute | solution.py:12
  272.4 12.6 %collective-permute-start.64 = (bf16[16,128]{1,0:T(8,128)(2,1)S(1)}, bf16[16,128]{1,0:T(8,128)(2,1)S(1)}, u32[]{:S(2)}, u32[]{:S(2)}) collective-permute-start(bf16[16,128]{1,0:T(8,128)(2,1)S(1)} %bitcast.396), channel_id=1, source_target_pairs={{0,14},{2,16},{4,18},{6,20},{8,22},{10,24},{12,26},{14,28},{16,30}... | collective-permute-start | bytes 12296 | tf_op jit(solution)/shard_map/ppermute | solution.py:12
  275.7 9.5 %collective-permute-start.67 = (bf16[16,128]{1,0:T(8,128)(2,1)S(1)}, bf16[16,128]{1,0:T(8,128)(2,1)S(1)}, u32[]{:S(2)}, u32[]{:S(2)}) collective-permute-start(bf16[16,128]{1,0:T(8,128)(2,1)S(1)} %bitcast.385), channel_id=1, source_target_pairs={{0,22},{2,24},{4,26},{6,28},{8,30},{10,0},{12,2},{14,4},{16,6},{18... | collective-permute-start | bytes 12296 | tf_op jit(solution)/shard_map/ppermute | solution.py:12
  275.7 9.4 %collective-permute-start.66 = (bf16[16,128]{1,0:T(8,128)(2,1)S(1)}, bf16[16,128]{1,0:T(8,128)(2,1)S(1)}, u32[]{:S(2)}, u32[]{:S(2)}) collective-permute-start(bf16[16,128]{1,0:T(8,128)(2,1)S(1)} %bitcast.386), channel_id=1, source_target_pairs={{0,10},{2,12},{4,14},{6,16},{8,18},{10,20},{12,22},{14,24},{16,26}... | collective-permute-start | bytes 12296 | tf_op jit(solution)/shard_map/ppermute | solution.py:12
  278.1 7.4 %collective-permute-start.68 = (bf16[1,16,128]{2,0,1:T(2,128)(2,1)S(1)}, bf16[1,16,128]{2,0,1:T(2,128)(2,1)S(1)}, u32[]{:S(2)}, u32[]{:S(2)}) collective-permute-start(bf16[1,16,128]{2,0,1:T(2,128)(2,1)S(1)} %get-tuple-element.14), channel_id=1, source_target_pairs={{0,1},{2,3},{4,5},{6,7},{8,9},{10,11},{12,13},{14,15},{16,17},{18,... | collective-permute-start | bytes 12296 | tf_op jit(solution)/shard_map/ppermute | solution.py:22
  (11 other events, 533.0 us)
where the time goes:
time: 326 us; the launch traced here: 324 us
  blocking collectives  157 us (48%)
  starting transfers between devices  148 us (45%)
  matrix products  8.11 us (2%)
  other arithmetic  5.32 us (2%)
    ppermute x60, starting transfers between devices, from_behind(): lax.ppermute(array, axis, [(i, (i + by) % devices) for i in range(devices)])  114 us
    all_gather x2, blocking collectives, gather_coarse(): lax.all_gather(restricted[None], ('fine', 'coarse'), axis=0, tiled=True)  82 us
    psum x2, blocking collectives, body(): totals = lax.psum(partials, ('fine', 'coarse'))  75.1 us
    ppermute x5, starting transfers between devices, with_halo(): after = lax.ppermute(leading, axis, down)  27.7 us
  transfers between devices with their start and end apart: 70, of which 4 were waited for; matrix products, arithmetic and copies ran while one was open for 1% of the time, Pallas kernels for 0%

commit v1 on v0

v1 whole, which is shorter than its diff:
```python
import jax
import jax.numpy as jnp
from jax import lax
from jax.sharding import PartitionSpec as P

PLANES = 6
ITERS = 2
AXES = ("fine", "coarse")
HIGHEST = lax.Precision.HIGHEST


def body(load_cases, dual_ops, coarse_basis, factor_blocks, pattern, partners, row_counts):
    cases, width = load_cases.shape[1:]
    blocks = PLANES + 2
    block_rows = width // blocks
    modes = coarse_basis.shape[1]
    terms = factor_blocks.shape[1]
    fine_count = lax.axis_size("fine")
    coarse_count = lax.axis_size("coarse")
    subs = fine_count * coarse_count
    fine_index = lax.axis_index("fine")
    coarse_index = lax.axis_index("coarse")
    me = fine_index * coarse_count + coarse_index

    partner_row = partners[0]
    below = jnp.where(coarse_index > 0, me - 1, -1)
    above = jnp.where(coarse_index < coarse_count - 1, me + 1, -1)
    facing = jnp.concatenate([partner_row * coarse_count + coarse_index, jnp.stack([below, above])])
    everyone = jnp.arange(subs, dtype=jnp.int32)
    chosen = facing[:, None] == everyone[None, :]
    selector = chosen.astype(jnp.bfloat16)

    plane_signs = jnp.where(fine_index < partner_row, 1.0, -1.0).astype(jnp.float32)
    block_signs = jnp.concatenate([plane_signs, jnp.array([-1.0, 1.0], jnp.float32)])
    signs = jnp.repeat(block_signs, block_rows)[None, :]
    live = (
        (jnp.arange(block_rows, dtype=jnp.int32)[None, :] < row_counts[0][:, None])
        .astype(jnp.float32)
        .reshape(1, width)
    )
    basis = coarse_basis[0]

    def by_block(values):
        return jnp.transpose(values.reshape(values.shape[0], blocks, block_rows), (1, 0, 2))

    def exchange(per_block):
        rows = per_block.shape[1]
        flat = per_block.reshape(blocks, rows * block_rows)
        out = jnp.dot(selector.T, flat, preferred_element_type=jnp.float32).astype(jnp.bfloat16)
        out = out.reshape(subs, rows, block_rows)
        arrived = lax.all_to_all(out, AXES, 0, 0, tiled=True).reshape(subs, rows * block_rows)
        back = jnp.dot(selector, arrived, preferred_element_type=jnp.float32).astype(jnp.bfloat16)
        return back.reshape(blocks, rows, block_rows)

    def to_rows(per_block):
        return jnp.transpose(per_block, (1, 0, 2)).reshape(per_block.shape[1], width)

    def gather(values):
        copies = jnp.broadcast_to(values[None], (subs,) + values.shape)
        return lax.all_to_all(copies, AXES, 0, 0, tiled=True)

    flat_factors = factor_blocks[0].reshape(-1, block_rows)
    pattern_rows = jnp.zeros((8, block_rows), jnp.float32)
    pattern_rows = pattern_rows.at[0, :terms].set(pattern[0].astype(jnp.float32))
    packed = jnp.concatenate([flat_factors, pattern_rows], axis=0)
    packed_all = lax.all_gather(packed, AXES, axis=0, tiled=False)
    who = jnp.concatenate([me[None], jnp.maximum(facing, 0)])
    packed_near = packed_all[who]
    factor_rows = flat_factors.shape[0]
    near_factors = packed_near[:, :factor_rows].reshape(blocks + 1, terms * modes, modes)
    near_pattern = packed_near[:, factor_rows, :terms].astype(jnp.int32)

    loads = load_cases[0]
    received = exchange(jnp.concatenate([by_block(loads), by_block(basis)], axis=1))
    facing_basis = received[:, cases:]
    near_basis = jnp.concatenate([basis[None, :, :block_rows], facing_basis], axis=0)[1:]
    residual = live * (loads.astype(jnp.float32) - to_rows(received[:, :cases]).astype(jnp.float32))

    def restrict(values):
        return lax.dot_general(
            values, basis.astype(jnp.float32), (((1,), (1,)), ((), ())), precision=HIGHEST
        )

    def coarse_direction(residual, restricted):
        picked = jnp.transpose(restricted[near_pattern], (0, 2, 1, 3))
        picked = picked.reshape(blocks + 1, cases, terms * modes)
        solved = jnp.einsum("jlk,jkb->jlb", picked, near_factors, precision=HIGHEST)
        solved = solved.astype(jnp.bfloat16)
        mine = jnp.dot(solved[0], basis, preferred_element_type=jnp.float32).astype(jnp.bfloat16)
        theirs = jnp.einsum(
            "jla,jam->jlm", solved[1:], near_basis, preferred_element_type=jnp.float32
        ).astype(jnp.bfloat16)
        return residual + live * (mine.astype(jnp.float32) - to_rows(theirs).astype(jnp.float32))

    def apply_dual(direction):
        return jnp.dot(
            direction.astype(jnp.bfloat16), dual_ops[0], preferred_element_type=jnp.float32
        ).astype(jnp.bfloat16)

    def image_of(applied):
        other = to_rows(exchange(by_block(applied)))
        return live * (applied.astype(jnp.float32) - other.astype(jnp.float32))

    def partial_sums(residual, direction, applied):
        gamma = jnp.sum(residual * direction, axis=1)
        delta = 2.0 * jnp.sum(direction * applied.astype(jnp.float32), axis=1)
        return jnp.stack([gamma, delta], axis=1)

    multipliers = jnp.zeros_like(residual)
    restricted = gather(restrict(residual))
    for iteration in range(ITERS):
        direction = coarse_direction(residual, restricted)
        applied = apply_dual(direction)
        sums = partial_sums(residual, direction, applied)
        image = image_of(applied)
        if iteration + 1 < ITERS:
            message = jnp.concatenate([restrict(image), sums], axis=1)
        else:
            message = sums
        collected = gather(message)
        totals = jnp.sum(collected[:, :, -2:], axis=0)
        step = (totals[:, 0] / totals[:, 1])[:, None]
        multipliers = multipliers + step * direction
        residual = residual - step * image
        if iteration + 1 < ITERS:
            restricted = restricted - step[None] * collected[:, :, :modes]
    return ((signs * multipliers)[None], (signs * residual)[None])


def solution(mesh):
    rows = P(AXES, None, None)
    return jax.shard_map(
        body,
        mesh=mesh,
        in_specs=(rows, rows, rows, P(AXES, None, None, None), P(AXES, None), P(AXES, None), P(AXES, None)),
        out_specs=(rows, rows),
        check_vma=False,
    )
```

time: 326 us -> 155 us (0.48)
  blocking collectives: 157 us -> 0 us
  starting transfers between devices: 148 us -> 22.3 us
  waiting for transfers between devices: 1.65 us -> 70.1 us
  local copies, waits for them, and re-layouts: 2.36 us -> 26.6 us
  between operations: 1.86 us -> 14.4 us
  other arithmetic: 5.32 us -> 12.7 us
    ppermute x70 -> x0, starting transfers between devices: 148 us -> none  [the longest x60 114 us: from_behind(): lax.ppermute(array, axis, [(i, (i + by) % devices) for i in range(devices)])]
    all_gather x2 -> x0, blocking collectives: 82 us -> none  [gather_coarse(): lax.all_gather(restricted[None], ('fine', 'coarse'), axis=0, tiled=True)]
    psum x2 -> x0, blocking collectives: 75.1 us -> none  [body(): totals = lax.psum(partials, ('fine', 'coarse'))]
    all_to_all x0 -> x6, waiting for transfers between devices: none -> 52 us  [the longest x3 31.6 us: exchange(): lax.all_to_all(out, AXES, 0, 0, tiled=True).reshape(subs, rows * block_rows)]
    all_to_all x0 -> x6, starting transfers between devices: none -> 22.3 us  [the longest x3 13.2 us: exchange(): lax.all_to_all(out, AXES, 0, 0, tiled=True).reshape(subs, rows * block_rows)]
    all_gather x0 -> x1, waiting for transfers between devices: none -> 18.1 us  [body(): packed_all = lax.all_gather(packed, AXES, axis=0, tiled=False)]
    unnamed x45 -> x36, local copies, waits for them, and re-layouts: 0.19 us -> 11.3 us
    gather x2 -> x3, local copies, waits for them, and re-layouts: 1.1 us -> 4.75 us  [the longest x2 2.87 us: coarse_direction(): picked = jnp.transpose(restricted[near_pattern], (0, 2, 1, 3))]
  transfers between devices with their start and end apart: 70 -> 7, of which waited for: 4 -> 7; matrix products, arithmetic and copies ran while one was open for 1% -> 7% of each run, Pallas kernels for 0% -> 0%
where the time goes in v1:
time: 155 us; the launch traced here: 153 us
  waiting for transfers between devices  70.1 us (45%)
  local copies, waits for them, and re-layouts  26.6 us (17%)
  starting transfers between devices  22.3 us (14%)
  between operations  14.4 us (9%)
  other arithmetic  12.7 us (8%)
  matrix products  7.08 us (5%)
    all_to_all x3, waiting for transfers between devices, exchange(): lax.all_to_all(out, AXES, 0, 0, tiled=True).reshape(subs, rows * block_rows)  31.6 us
    all_to_all x3, waiting for transfers between devices, gather(): return lax.all_to_all(copies, AXES, 0, 0, tiled=True)  20.4 us
    all_gather x1, waiting for transfers between devices, body(): packed_all = lax.all_gather(packed, AXES, axis=0, tiled=False)  18.1 us
    all_to_all x3, starting transfers between devices, exchange(): lax.all_to_all(out, AXES, 0, 0, tiled=True).reshape(subs, rows * block_rows)  13.2 us
    unnamed x36, local copies, waits for them, and re-layouts  11.3 us
    all_to_all x3, starting transfers between devices, gather(): return lax.all_to_all(copies, AXES, 0, 0, tiled=True)  9.04 us
    all_to_all x2, other arithmetic, gather(): return lax.all_to_all(copies, AXES, 0, 0, tiled=True)  3.25 us
  transfers between devices with their start and end apart: 7, of which 7 were waited for; matrix products, arithmetic and copies ran while one was open for 7% of the time, Pallas kernels for 0%

profile of v1, /device:TPU:1, one launch (start us, length us, event | category | flops | bytes accessed | tf_op | source)
XLA Modules:
  0.0 153.3 jit_solution(7039155157948089024)
XLA Ops:
  7.2 0.8 convert_element_type.181
  8.0 1.0 reshape_squeeze.11
  9.1 0.6 select_maximum_fusion
  9.7 0.8 copy.96
  10.5 0.9 copy.97
  11.4 0.7 add_bitcast_fusion
  12.2 0.4 fusion.4
  12.6 0.9 copy.98
  13.5 7.1 %all-to-all-start = ((bf16[32,64,128]{2,1,0:T(8,128)(2,1)}), bf16[32,64,128]{2,1,0:T(8,128)(2,1)S(1)}, u32[]{:S(2)}, u32[]{:S(2)}) async-start(bf16[32,64,128]{2,1,0:T(8,128)(2,1)} %bitcast.62), calls=%async_computation | async-start | bytes 1048576 | tf_op jit(solution)/shard_map/all_to_all | solution.py:51
  20.7 16.0 %all-to-all-done = bf16[32,64,128]{2,1,0:T(8,128)(2,1)S(1)} async-done(((bf16[32,64,128]{2,1,0:T(8,128)(2,1)}), bf16[32,64,128]{2,1,0:T(8,128)(2,1)S(1)}, u32[]{:S(2)}, u32[]{:S(2)}) %all-to-all-start) | async-done | bytes 524320 | tf_op jit(solution)/shard_map/all_to_all | solution.py:51
  36.6 0.4 fusion.7
  37.3 0.9 reshape.387
  38.2 3.4 %all-to-all-start.1 = ((f32[32,1,768]{2,1,0:T(1,128)}), f32[32,1,768]{2,1,0:T(1,128)S(1)}, u32[]{:S(2)}, u32[]{:S(2)}) async-start(f32[32,1,768]{2,1,0:T(1,128)} %reshape.387), calls=%async_computation.1 | async-start | bytes 196608 | tf_op jit(solution)/shard_map/all_to_all | solution.py:60
  41.7 7.9 %all-to-all-done.1 = f32[32,1,768]{2,1,0:T(1,128)S(1)} async-done(((f32[32,1,768]{2,1,0:T(1,128)}), f32[32,1,768]{2,1,0:T(1,128)S(1)}, u32[]{:S(2)}, u32[]{:S(2)}) %all-to-all-start.1) | async-done | bytes 98336 | tf_op jit(solution)/shard_map/all_to_all | solution.py:60
  49.6 0.5 broadcast.156
  50.2 0.8 reduce.2
  51.0 0.1 reshape.388
  51.2 18.1 %all-gather.3.cloned.1.call-done = f32[2560,128]{1,0:T(8,128)} async-done(((f32[80,128]{1,0:T(8,128)}), f32[2560,128]{1,0:T(8,128)}) %all-gather.3.cloned.1.call-update) | async-done | bytes 1310736 | tf_op jit(solution)/shard_map/all_gather | solution.py:66
  69.2 1.9 %gather_fusion = f32[9,80,128]{2,1,0:T(8,128)S(1)} fusion(f32[32,80,128]{2,1,0:T(8,128)} %bitcast.203, s32[1024]{0:T(1024)S(1)} %pad_clamp_fusion.1), kind=kCustom, calls=%fused_computation | custom fusion | bytes 737316 | tf_op jit(solution)/shard_map/gather | solution.py:68
  71.1 0.7 slice.80
  72.2 0.6 gather_fusion.1
  72.9 0.8 reshape.339
  73.7 1.3 reshape.340
  75.0 1.7 %convolution_convert_fusion.7 = bf16[9,16,48]{2,1,0:T(8,128)(2,1)S(1)} fusion(f32[9,16,192]{2,1,0:T(8,128)} %reshape.339, f32[9,192,48]{2,1,0:T(8,128)S(1)} %reshape.340), kind=kOutput, calls=%fused_computation.18 | convolution fusion | flops 15932160 | bytes 456192 | tf_op jit(solution)/shard_map/jlk,jkb->jlb/dot_general | solution.py:87
  76.8 0.1 fusion.17
  76.9 0.1 fusion.25
  77.1 0.6 copy-done.3
  77.7 0.5 multiply_reduce_fusion.1
  78.2 0.3 fusion.5
  78.5 0.7 copy.102
  79.2 3.6 %all-to-all-start.2 = ((bf16[32,16,128]{2,1,0:T(8,128)(2,1)}), bf16[32,16,128]{2,1,0:T(8,128)(2,1)}, u32[]{:S(2)}, u32[]{:S(2)}) async-start(bf16[32,16,128]{2,1,0:T(8,128)(2,1)} %bitcast.196), calls=%async_computation.2 | async-start | bytes 262144 | tf_op jit(solution)/shard_map/all_to_all | solution.py:51
  82.9 0.7 copy.81
  83.6 7.5 %all-to-all-done.2 = bf16[32,16,128]{2,1,0:T(8,128)(2,1)} async-done(((bf16[32,16,128]{2,1,0:T(8,128)(2,1)}), bf16[32,16,128]{2,1,0:T(8,128)(2,1)}, u32[]{:S(2)}, u32[]{:S(2)}) %all-to-all-start.2) | async-done | bytes 131104 | tf_op jit(solution)/shard_map/all_to_all | solution.py:51
  91.1 1.1 fusion.27
  92.2 0.1 fusion.40
  92.3 0.8 pad_maximum_fusion
  93.1 0.7 broadcast_in_dim.24
  93.8 1.9 %reshape.389 = f32[32,1,800]{2,1,0:T(1,128)} reshape(f32[32,16,50]{2,1,0:T(8,128)} %broadcast_in_dim.24) | data formatting | bytes 204800
  95.7 3.1 %all-to-all-start.3 = ((f32[32,1,800]{2,1,0:T(1,128)}), f32[32,1,800]{2,1,0:T(1,128)}, u32[]{:S(2)}, u32[]{:S(2)}) async-start(f32[32,1,800]{2,1,0:T(1,128)} %reshape.389), calls=%async_computation.3 | async-start | bytes 229376 | tf_op jit(solution)/shard_map/all_to_all | solution.py:60
  98.8 0.7 fusion.74
  99.5 1.2 pad_maximum_fusion.2
  100.7 6.2 %all-to-all-done.3 = f32[32,1,800]{2,1,0:T(1,128)} async-done(((f32[32,1,800]{2,1,0:T(1,128)}), f32[32,1,800]{2,1,0:T(1,128)}, u32[]{:S(2)}, u32[]{:S(2)}) %all-to-all-start.3) | async-done | bytes 102432 | tf_op jit(solution)/shard_map/all_to_all | solution.py:60
  106.9 2.4 %reduce.3 = f32[32,800]{1,0:T(8,128)} reduce(f32[32,1,800]{2,1,0:T(1,128)} %all-to-all-done.3, f32[]{:T(128)} %broadcast.156), dimensions={1}, to_apply=%all_to_all.21.reduce_sub_computation | reduce | bytes 204804 | tf_op jit(solution)/shard_map/all_to_all | solution.py:60
  109.4 1.8 %reshape.390 = f32[32,16,50]{2,1,0:T(8,128)} reshape(f32[32,800]{1,0:T(8,128)} %reduce.3) | data formatting | bytes 204800
  111.2 1.1 slice_reduce_fusion
  112.2 0.7 fusion.78
  112.9 1.3 copy.93
  114.2 0.6 copy.92
  114.8 0.7 divide_bitcast_fusion
  115.5 1.8 %fusion.32 = f32[32,16,48]{2,1,0:T(8,128)} fusion(f32[32,16,48]{2,1,0:T(8,128)S(1)} %reshape.388, f32[32,16,50]{2,1,0:T(8,128)} %reshape.390, f32[16]{0:T(128)S(1)} %divide_bitcast_fusion), kind=kLoop, calls=%fused_computation.44 | loop fusion | flops 49152 | bytes 294976 | tf_op jit(solution)/shard_map/sub | solution.py:126
  117.3 2.3 %gather_fusion.2 = f32[36,16,48]{2,1,0:T(8,128)} fusion(f32[32,16,48]{2,1,0:T(8,128)} %fusion.32, s32[1024]{0:T(1024)S(1)} %pad_clamp_fusion), kind=kCustom, calls=%fused_computation.2 | custom fusion | bytes 221328 | tf_op jit(solution)/shard_map/gather | solution.py:85
  119.6 1.8 %copy.84 = f32[9,16,4,48]{3,2,1,0:T(4,128)} copy(f32[9,16,4,48]{3,1,2,0:T(8,128)} %bitcast.186) | data formatting | bytes 221184 | tf_op jit(solution)/shard_map/transpose | solution.py:85
  121.4 1.1 reshape.345
  122.5 0.8 convolution_convert_fusion.6
  123.7 0.5 multiply_reduce_fusion
  124.2 0.6 broadcast_in_dim.25
  124.8 2.5 %all-to-all-start.4 = ((f32[32,16,2]{1,2,0:T(2,128)}), f32[32,16,2]{1,2,0:T(2,128)S(1)}, u32[]{:S(2)}, u32[]{:S(2)}) async-start(f32[32,16,2]{1,2,0:T(2,128)} %broadcast_in_dim.25), calls=%async_computation.4 | async-start | bytes 65536 | tf_op jit(solution)/shard_map/all_to_all | solution.py:60
  127.4 0.3 fusion.6
  127.7 0.7 copy.106
  128.3 6.3 %all-to-all-done.4 = f32[32,16,2]{1,2,0:T(2,128)S(1)} async-done(((f32[32,16,2]{1,2,0:T(2,128)}), f32[32,16,2]{1,2,0:T(2,128)S(1)}, u32[]{:S(2)}, u32[]{:S(2)}) %all-to-all-start.4) | async-done | bytes 4128 | tf_op jit(solution)/shard_map/all_to_all | solution.py:60
  134.6 2.6 %all-to-all-start.5 = ((bf16[32,16,128]{2,1,0:T(8,128)(2,1)}), bf16[32,16,128]{2,1,0:T(8,128)(2,1)S(1)}, u32[]{:S(2)}, u32[]{:S(2)}) async-start(bf16[32,16,128]{2,1,0:T(8,128)(2,1)} %bitcast.80), calls=%async_computation.5 | async-start | bytes 262144 | tf_op jit(solution)/shard_map/all_to_all | solution.py:51
  137.3 8.2 %all-to-all-done.5 = bf16[32,16,128]{2,1,0:T(8,128)(2,1)S(1)} async-done(((bf16[32,16,128]{2,1,0:T(8,128)(2,1)}), bf16[32,16,128]{2,1,0:T(8,128)(2,1)S(1)}, u32[]{:S(2)}, u32[]{:S(2)}) %all-to-all-start.5) | async-done | bytes 131104 | tf_op jit(solution)/shard_map/all_to_all | solution.py:51
  145.5 0.2 fusion.29
  145.7 0.7 fusion.54
  (51 shorter events, 1.6 us)
Async XLA Ops:
  7.2 70.5 %copy-start = (bf16[1,1024,1024]{2,1,0:T(8,128)(2,1)S(1)}, bf16[1,1024,1024]{2,1,0:T(8,128)(2,1)}, u32[]{:S(2)}) copy-start(bf16[1,1024,1024]{2,1,0:T(8,128)(2,1)} %param.11) | copy-start | bytes 6291460
  7.2 13.4 %copy-start.9 = (s32[1,8]{1,0:T(1,128)S(1)}, s32[1,8]{1,0:T(1,128)}, u32[]{:S(2)}) copy-start(s32[1,8]{1,0:T(1,128)} %param.16) | copy-start | bytes 100
  7.2 62.0 %all-gather.3.cloned.1.call-start = ((), (), s32[]{:S(2)}) async-start(), calls=%async_computation.6 | async-start | bytes 1351680 | tf_op jit(solution)/shard_map/all_gather | solution.py:66
  9.0 28.0 %copy-start.1 = (bf16[1,48,1024]{2,1,0:T(8,128)(2,1)S(1)}, bf16[1,48,1024]{2,1,0:T(8,128)(2,1)}, u32[]{:S(2)}) copy-start(bf16[1,48,1024]{2,1,0:T(8,128)(2,1)} %param.12) | copy-start | bytes 294916
  9.0 28.0 %copy-start.2 = (bf16[1,16,1024]{2,1,0:T(8,128)(2,1)S(1)}, bf16[1,16,1024]{2,1,0:T(8,128)(2,1)}, u32[]{:S(2)}) copy-start(bf16[1,16,1024]{2,1,0:T(8,128)(2,1)} %param.10) | copy-start | bytes 98308
  12.2 66.1 %copy-start.7 = (s32[8]{0:T(128)}, s32[8]{0:T(128)S(1)}, u32[]{:S(2)}) copy-start(s32[8]{0:T(128)S(1)} %get-tuple-element.19) | copy-start | bytes 100
  13.5 23.1 %all-to-all-start = ((bf16[32,64,128]{2,1,0:T(8,128)(2,1)}), bf16[32,64,128]{2,1,0:T(8,128)(2,1)S(1)}, u32[]{:S(2)}, u32[]{:S(2)}) async-start(bf16[32,64,128]{2,1,0:T(8,128)(2,1)} %bitcast.62), calls=%async_computation | async-start | bytes 1048576 | tf_op jit(solution)/shard_map/all_to_all | solution.py:51
  38.2 11.4 %all-to-all-start.1 = ((f32[32,1,768]{2,1,0:T(1,128)}), f32[32,1,768]{2,1,0:T(1,128)S(1)}, u32[]{:S(2)}, u32[]{:S(2)}) async-start(f32[32,1,768]{2,1,0:T(1,128)} %reshape.387), calls=%async_computation.1 | async-start | bytes 196608 | tf_op jit(solution)/shard_map/all_to_all | solution.py:60
  41.7 35.1 %copy-start.5 = (bf16[8,48,128]{2,0,1:T(8,128)(2,1)}, bf16[8,48,128]{2,0,1:T(8,128)(2,1)S(1)}, u32[]{:S(2)}) copy-start(bf16[8,48,128]{2,0,1:T(8,128)(2,1)S(1)} %slice.82) | copy-start | bytes 294916
  77.1 0.6 copy-start.3
  79.2 11.8 %all-to-all-start.2 = ((bf16[32,16,128]{2,1,0:T(8,128)(2,1)}), bf16[32,16,128]{2,1,0:T(8,128)(2,1)}, u32[]{:S(2)}, u32[]{:S(2)}) async-start(bf16[32,16,128]{2,1,0:T(8,128)(2,1)} %bitcast.196), calls=%async_computation.2 | async-start | bytes 262144 | tf_op jit(solution)/shard_map/all_to_all | solution.py:51
  95.7 11.2 %all-to-all-start.3 = ((f32[32,1,800]{2,1,0:T(1,128)}), f32[32,1,800]{2,1,0:T(1,128)}, u32[]{:S(2)}, u32[]{:S(2)}) async-start(f32[32,1,800]{2,1,0:T(1,128)} %reshape.389), calls=%async_computation.3 | async-start | bytes 229376 | tf_op jit(solution)/shard_map/all_to_all | solution.py:60
  117.3 6.1 %copy-start.6 = (bf16[8,48,128]{2,0,1:T(8,128)(2,1)S(1)}, bf16[8,48,128]{2,0,1:T(8,128)(2,1)}, u32[]{:S(2)}) copy-start(bf16[8,48,128]{2,0,1:T(8,128)(2,1)} %copy-done.5) | copy-start | bytes 294916
  122.5 4.8 %copy-start.8 = (s32[8]{0:T(128)S(1)}, s32[8]{0:T(128)}, u32[]{:S(2)}) copy-start(s32[8]{0:T(128)} %copy-done.7) | copy-start | bytes 100
  122.5 14.7 %copy-start.10 = (f32[8]{0:T(128)S(1)}, f32[8]{0:T(128)}, u32[]{:S(2)}) copy-start(f32[8]{0:T(128)} %pad_maximum_fusion.2) | copy-start | bytes 100
  123.4 22.3 %copy-start.4 = (f32[16,1024]{1,0:T(8,128)S(1)}, f32[16,1024]{1,0:T(8,128)}, u32[]{:S(2)}) copy-start(f32[16,1024]{1,0:T(8,128)} %copy-done.3) | copy-start | bytes 196612
  124.8 9.8 %all-to-all-start.4 = ((f32[32,16,2]{1,2,0:T(2,128)}), f32[32,16,2]{1,2,0:T(2,128)S(1)}, u32[]{:S(2)}, u32[]{:S(2)}) async-start(f32[32,16,2]{1,2,0:T(2,128)} %broadcast_in_dim.25), calls=%async_computation.4 | async-start | bytes 65536 | tf_op jit(solution)/shard_map/all_to_all | solution.py:60
  134.6 10.9 %all-to-all-start.5 = ((bf16[32,16,128]{2,1,0:T(8,128)(2,1)}), bf16[32,16,128]{2,1,0:T(8,128)(2,1)S(1)}, u32[]{:S(2)}, u32[]{:S(2)}) async-start(bf16[32,16,128]{2,1,0:T(8,128)(2,1)} %bitcast.80), calls=%async_computation.5 | async-start | bytes 262144 | tf_op jit(solution)/shard_map/all_to_all | solution.py:51
Sparse Core Ops, SparseCore 0:
  11.5 57.7 all-gather.2
